TPU v7x, 128 devices: a whole 4x4x4 slice. The times are simulated.
128 devices in a mesh: year: 4 (over z_lo, core), tile: 32 (over x, z_hi, y).
Axes of the slice: x: 4, y: 4, z: 4 (z_hi: 2, z_lo: 2; z = z_hi * 2 + z_lo), core: 2. Of those that a mesh axis runs over, the one named last changes fastest.
Arguments:
- station_tile: int32 [131072, 1], P(('year', 'tile')), may hold values from 0 to 31; in each aligned block of 1024 rows (0 to 1023, 1024 to 2047, ...) at most 96 rows name the same one
- station_cell: int32 [131072], P(('year', 'tile')), may hold values from 0 to 262143
- station_value: float32 [131072], P(('year', 'tile')), may hold values from -6 to 6
- class_ids: int32 [128, 8192], P(None, 'tile'), may hold values from 0 to 15
- coeff_table: float32 [3, 16], replicated, may hold values from 0.2 to 2
- lag_blocks: float32 [5, 128, 128], replicated, may hold values from -0.5 to 0.5
Outputs:
- filtered: float32 [32, 128, 8192], P('year', None, 'tile')
Inputs may be any that keep to these rules, and one draw needn't show every extreme that they name: `station_tile`: in the rows of one device no tile is named by more than 96 rows, a bound that some block reaches.
All inputs are finite; a program needn't handle non-finite values.
Results may differ from a plain program's by a relative error of at most 0.00013.
Values sent between devices are 32-bit elements; how exact they have to be, the bound alone decides.
A program may use at most 192 MiB of HBM per device.

v0:
```python
import jax
import jax.numpy as jnp
from jax import lax
from jax.sharding import PartitionSpec as P

DAY_DEV = 8


def with_halo(block, sides, width):
    for axis, dim in sides:
        count = lax.axis_size(axis)
        forward = [(i, i + 1) for i in range(count - 1)]
        forward.append((count - 1, 0))
        backward = [(target, source) for source, target in forward]
        low = lax.ppermute(
            lax.slice_in_dim(block, block.shape[dim] - width, None, axis=dim), axis, forward
        )
        high = lax.ppermute(lax.slice_in_dim(block, 0, width, axis=dim), axis, backward)
        block = jnp.concatenate([low, block, high], axis=dim)
    return block


def apply_ext(extended, kappa, hzon, hmer):
    centre = extended[:, :, 1:-1]
    east = extended[:, :, 2:]
    west = extended[:, :, :-2]
    zeros_row = jnp.zeros_like(centre[:, :1, :])
    north = jnp.concatenate([centre[:, 1:, :], zeros_row], axis=1)
    south = jnp.concatenate([zeros_row, centre[:, :-1, :]], axis=1)
    return (
        kappa * centre + hzon * (2.0 * centre - east - west) + hmer * (2.0 * centre - north - south)
    )


def body(station_tile, station_cell, station_value, class_ids, coeff_table, lag_blocks):
    ntiles = lax.axis_size("tile")
    lat_rows = class_ids.shape[0]
    lon_cols = class_ids.shape[1]
    plane = lat_rows * lon_cols
    whole = DAY_DEV * plane
    target = station_tile[:, 0]
    capacity = 3 * station_value.shape[0] // ntiles
    onehot = (target[:, None] == jnp.arange(ntiles, dtype=jnp.int32)[None, :]).astype(jnp.int32)
    running = jnp.cumsum(onehot, axis=0)
    slot_of = jnp.sum(running * onehot, axis=1) - 1
    position = target * capacity + slot_of
    send_value = (
        jnp.zeros((ntiles * capacity,), jnp.float32)
        .at[position]
        .set(station_value)
        .reshape(ntiles, capacity)
    )
    send_cell = (
        jnp.full((ntiles * capacity,), -1, jnp.int32)
        .at[position]
        .set(station_cell)
        .reshape(ntiles, capacity)
    )
    recv_value, recv_cell = (
        lax.all_to_all(send_value, "tile", split_axis=0, concat_axis=0, tiled=True),
        lax.all_to_all(send_cell, "tile", split_axis=0, concat_axis=0, tiled=True),
    )
    recv_cell = recv_cell.reshape(-1)
    flat_index = jnp.where(recv_cell >= 0, recv_cell, whole)
    residual_field = (
        jnp.zeros((whole,), jnp.float32).at[flat_index].add(recv_value.reshape(-1), mode="drop")
    )
    residual_field = residual_field.reshape(DAY_DEV, lat_rows, lon_cols)
    classes = jnp.arange(coeff_table.shape[1], dtype=jnp.int32)
    selector = (class_ids[None, :, :] == classes[:, None, None]).astype(jnp.float32)
    coeffs = jnp.einsum("cn,nij->cij", coeff_table, selector, precision=lax.Precision.HIGHEST)
    current = residual_field
    for sweep in range(2):
        extended = with_halo(current, (("tile", 2),), 1)
        current = apply_ext(extended, coeffs[0], coeffs[1], coeffs[2])
    days_ext = with_halo(current, (("year", 0),), 2)
    filtered = jnp.zeros_like(current)
    for k in range(5):
        window = days_ext[k : k + DAY_DEV]
        filtered = filtered + jnp.einsum(
            "ij,djk->dik", lag_blocks[k], window, precision=lax.Precision.HIGHEST
        )
    return filtered


def solution(mesh):
    in_specs = (
        P(("year", "tile"), None),
        P(("year", "tile")),
        P(("year", "tile")),
        P(None, "tile"),
        P(),
        P(),
    )
    out_specs = P("year", None, "tile")
    return jax.shard_map(body, mesh=mesh, in_specs=in_specs, out_specs=out_specs, check_vma=False)
```

profile of v0, /device:TPU:1, one launch (start us, length us, event | category | flops | bytes accessed | tf_op | source)
XLA Modules:
  0.0 106.8 jit_solution(16969770166342769310)
XLA Ops:
  0.0 0.8 fusion.22
  0.8 9.0 %reduce-window.6 = s32[32,8,128]{2,1,0:T(8,128)S(1)} reduce-window(s32[32,8,128]{2,1,0:T(8,128)S(1)} %fusion.22, s32[]{:T(128)} %constant.10.clone.1), window={size=1x1x128 pad=0_0x0_0x127_0}, to_apply=%region_0.0 | reduce-window | flops 4161536 | bytes 262148 | tf_op jit(solution)/shard_map/reduce-window
  10.3 4.5 %scatter_custom_fusion = s32[3072]{0:T(1024)S(1)} fusion(s32[1024]{0:T(1024)S(1)} %bitcast.62, s32[1024]{0:T(1024)} %param.7, s32[]{:T(128)} %constant.8.clone.1), kind=kCustom, calls=%fused_computation.55 | custom fusion | bytes 12800 | tf_op jit(solution)/shard_map/scatter | solution.py:56
  15.5 11.2 %all-to-all-start = ((s32[32,1,96]{2,1,0:T(1,128)}), s32[32,1,96]{2,1,0:T(1,128)S(1)}, u32[]{:S(2)}, u32[]{:S(2)}) async-start(s32[32,1,96]{2,1,0:T(1,128)} %all_to_all.12), calls=%async_computation | async-start | bytes 32768 | tf_op jit(solution)/shard_map/all_to_all | solution.py:61
  26.7 0.7 fusion.4
  27.7 4.5 %scatter_custom_fusion.1 = f32[3072]{0:T(1024)S(1)} fusion(s32[1024]{0:T(1024)S(1)} %bitcast.63, f32[1024]{0:T(1024)} %param.8, f32[]{:T(128)} %constant.7.clone.1), kind=kCustom, calls=%fused_computation.53 | custom fusion | bytes 12800 | tf_op jit(solution)/shard_map/scatter | solution.py:50
  33.2 2.1 %all-to-all-done = s32[32,1,96]{2,1,0:T(1,128)S(1)} async-done(((s32[32,1,96]{2,1,0:T(1,128)}), s32[32,1,96]{2,1,0:T(1,128)S(1)}, u32[]{:S(2)}, u32[]{:S(2)}) %all-to-all-start) | async-done | bytes 12320 | tf_op jit(solution)/shard_map/all_to_all | solution.py:61
  35.3 7.2 %all-to-all-start.1 = ((f32[32,1,96]{2,1,0:T(1,128)}), f32[32,1,96]{2,1,0:T(1,128)S(1)}, u32[]{:S(2)}, u32[]{:S(2)}) async-start(f32[32,1,96]{2,1,0:T(1,128)} %all_to_all.14), calls=%async_computation.1 | async-start | bytes 32768 | tf_op jit(solution)/shard_map/all_to_all | solution.py:60
  43.8 7.3 %all-to-all-done.1 = f32[32,1,96]{2,1,0:T(1,128)S(1)} async-done(((f32[32,1,96]{2,1,0:T(1,128)}), f32[32,1,96]{2,1,0:T(1,128)S(1)}, u32[]{:S(2)}, u32[]{:S(2)}) %all-to-all-start.1) | async-done | bytes 12320 | tf_op jit(solution)/shard_map/all_to_all | solution.py:60
  52.4 16.8 %scatter_custom_fusion.2 = f32[262144]{0:T(1024)S(1)} fusion(s32[3072]{0:T(1024)S(1)} %bitcast.61, f32[3072]{0:T(1024)S(1)} %reshape.97, f32[]{:T(128)} %constant.7.clone.1), kind=kCustom, calls=%fused_computation.30 | custom fusion | flops 3072 | bytes 1048580 | tf_op jit(solution)/shard_map/scatter-add | solution.py:66
  69.9 1.6 %collective-permute-start = (f32[8,128,1]{1,2,0:T(1,128)S(1)}, f32[8,128,1]{1,2,0:T(1,128)S(1)}, u32[]{:S(2)}, u32[]{:S(2)}) collective-permute-start(f32[8,128,1]{1,2,0:T(1,128)S(1)} %get-tuple-element.13), channel_id=1, source_target_pairs={{1,0},{2,1},{3,2},{4,3},{5,4},{6,5},{7,6},{8,7},{9,8},{10,9},{11,1... | collective-permute-start | bytes 12296 | tf_op jit(solution)/shard_map/ppermute | solution.py:18
  72.4 7.2 %collective-permute-done.1 = f32[8,128,1]{1,2,0:T(1,128)S(1)} collective-permute-done((f32[8,128,1]{1,2,0:T(1,128)S(1)}, f32[8,128,1]{1,2,0:T(1,128)S(1)}, u32[]{:S(2)}, u32[]{:S(2)}) %collective-permute-start.1) | collective-permute-done | bytes 4128 | tf_op jit(solution)/shard_map/ppermute | solution.py:15
  80.3 1.5 %collective-permute-start.3 = (f32[8,128,1]{1,2,0:T(1,128)S(1)}, f32[8,128,1]{1,2,0:T(1,128)S(1)}, u32[]{:S(2)}, u32[]{:S(2)}) collective-permute-start(f32[8,128,1]{1,2,0:T(1,128)S(1)} %get-tuple-element.10), channel_id=1, source_target_pairs={{0,1},{1,2},{2,3},{3,4},{4,5},{5,6},{6,7},{7,8},{8,9},{9,10},{10,1... | collective-permute-start | bytes 12296 | tf_op jit(solution)/shard_map/ppermute | solution.py:15
  82.1 0.9 collective-permute-done.2
  83.1 5.5 %collective-permute-done.3 = f32[8,128,1]{1,2,0:T(1,128)S(1)} collective-permute-done((f32[8,128,1]{1,2,0:T(1,128)S(1)}, f32[8,128,1]{1,2,0:T(1,128)S(1)}, u32[]{:S(2)}, u32[]{:S(2)}) %collective-permute-start.3) | collective-permute-done | bytes 4128 | tf_op jit(solution)/shard_map/ppermute | solution.py:15
  89.2 5.9 %collective-permute-start.4 = (f32[2,128,256]{1,2,0:T(8,128)S(1)}, f32[2,128,256]{1,2,0:T(8,128)S(1)}, u32[]{:S(2)}, u32[]{:S(2)}) collective-permute-start(f32[2,128,256]{1,2,0:T(8,128)S(1)} %get-tuple-element.5), channel_id=1, source_target_pairs={{0,32},{32,64},{64,96},{96,0},{1,33},{33,65},{65,97},{97,1},{2,34}... | collective-permute-start | bytes 786440 | tf_op jit(solution)/shard_map/ppermute | solution.py:15
  95.2 1.0 fusion.25
  96.2 3.8 %collective-permute-done.4 = f32[2,128,256]{1,2,0:T(8,128)S(1)} collective-permute-done((f32[2,128,256]{1,2,0:T(8,128)S(1)}, f32[2,128,256]{1,2,0:T(8,128)S(1)}, u32[]{:S(2)}, u32[]{:S(2)}) %collective-permute-start.4) | collective-permute-done | bytes 262176 | tf_op jit(solution)/shard_map/ppermute | solution.py:15
  100.0 1.0 fusion.6
  100.9 1.5 %collective-permute-done.5 = f32[2,128,256]{1,2,0:T(8,128)S(1)} collective-permute-done((f32[2,128,256]{1,2,0:T(8,128)S(1)}, f32[2,128,256]{1,2,0:T(8,128)S(1)}, u32[]{:S(2)}, u32[]{:S(2)}) %collective-permute-start.5) | collective-permute-done | bytes 262176 | tf_op jit(solution)/shard_map/ppermute | solution.py:18
  102.5 1.0 fusion.5
  103.5 1.0 fusion.1
  104.4 1.0 fusion.3
  105.5 1.3 %copy.24 = f32[8,128,256]{2,1,0:T(8,128)} copy(f32[8,128,256]{1,2,0:T(8,128)S(1)} %fusion.3) | data formatting | bytes 2097152 | tf_op jit(solution)/shard_map/add | solution.py:80
  (43 shorter events, 8.3 us)
Async XLA Ops:
  0.0 26.7 %copy-start = (f32[3,16]{1,0:T(4,128)S(1)}, f32[3,16]{1,0:T(4,128)}, u32[]{:S(2)}) copy-start(f32[3,16]{1,0:T(4,128)} %param.10) | copy-start | bytes 580
  0.0 10.2 %copy-start.3 = (s32[1024,1]{0,1:T(1,128)S(1)}, s32[1024,1]{0,1:T(1,128)}, u32[]{:S(2)}) copy-start(s32[1024,1]{0,1:T(1,128)} %param.6) | copy-start | bytes 12292
  0.0 26.7 %copy-start.2 = (s32[128,256]{1,0:T(8,128)S(1)}, s32[128,256]{1,0:T(8,128)}, u32[]{:S(2)}) copy-start(s32[128,256]{1,0:T(8,128)} %param.9) | copy-start | bytes 393220
  15.5 19.8 %all-to-all-start = ((s32[32,1,96]{2,1,0:T(1,128)}), s32[32,1,96]{2,1,0:T(1,128)S(1)}, u32[]{:S(2)}, u32[]{:S(2)}) async-start(s32[32,1,96]{2,1,0:T(1,128)} %all_to_all.12), calls=%async_computation | async-start | bytes 32768 | tf_op jit(solution)/shard_map/all_to_all | solution.py:61
  35.3 15.8 %all-to-all-start.1 = ((f32[32,1,96]{2,1,0:T(1,128)}), f32[32,1,96]{2,1,0:T(1,128)S(1)}, u32[]{:S(2)}, u32[]{:S(2)}) async-start(f32[32,1,96]{2,1,0:T(1,128)} %all_to_all.14), calls=%async_computation.1 | async-start | bytes 32768 | tf_op jit(solution)/shard_map/all_to_all | solution.py:60
  69.9 2.5 %collective-permute-start = (f32[8,128,1]{1,2,0:T(1,128)S(1)}, f32[8,128,1]{1,2,0:T(1,128)S(1)}, u32[]{:S(2)}, u32[]{:S(2)}) collective-permute-start(f32[8,128,1]{1,2,0:T(1,128)S(1)} %get-tuple-element.13), channel_id=1, source_target_pairs={{1,0},{2,1},{3,2},{4,3},{5,4},{6,5},{7,6},{8,7},{9,8},{10,9},{11,1... | collective-permute-start | bytes 12296 | tf_op jit(solution)/shard_map/ppermute | solution.py:18
  71.5 8.2 %collective-permute-start.1 = (f32[8,128,1]{1,2,0:T(1,128)S(1)}, f32[8,128,1]{1,2,0:T(1,128)S(1)}, u32[]{:S(2)}, u32[]{:S(2)}) collective-permute-start(f32[8,128,1]{1,2,0:T(1,128)S(1)} %get-tuple-element.14), channel_id=1, source_target_pairs={{0,1},{1,2},{2,3},{3,4},{4,5},{5,6},{6,7},{7,8},{8,9},{9,10},{10,1... | collective-permute-start | bytes 12296 | tf_op jit(solution)/shard_map/ppermute | solution.py:15
  80.3 2.8 %collective-permute-start.2 = (f32[8,128,1]{1,2,0:T(1,128)S(1)}, f32[8,128,1]{1,2,0:T(1,128)S(1)}, u32[]{:S(2)}, u32[]{:S(2)}) collective-permute-start(f32[8,128,1]{1,2,0:T(1,128)S(1)} %get-tuple-element.9), channel_id=1, source_target_pairs={{1,0},{2,1},{3,2},{4,3},{5,4},{6,5},{7,6},{8,7},{9,8},{10,9},{11,1... | collective-permute-start | bytes 12296 | tf_op jit(solution)/shard_map/ppermute | solution.py:18
  80.3 8.2 %collective-permute-start.3 = (f32[8,128,1]{1,2,0:T(1,128)S(1)}, f32[8,128,1]{1,2,0:T(1,128)S(1)}, u32[]{:S(2)}, u32[]{:S(2)}) collective-permute-start(f32[8,128,1]{1,2,0:T(1,128)S(1)} %get-tuple-element.10), channel_id=1, source_target_pairs={{0,1},{1,2},{2,3},{3,4},{4,5},{5,6},{6,7},{7,8},{8,9},{9,10},{10,1... | collective-permute-start | bytes 12296 | tf_op jit(solution)/shard_map/ppermute | solution.py:15
  89.2 6.0 %copy-start.1 = (f32[5,128,128]{2,1,0:T(8,128)S(1)}, f32[5,128,128]{2,1,0:T(8,128)}, u32[]{:S(2)}) copy-start(f32[5,128,128]{2,1,0:T(8,128)} %param.11) | copy-start | bytes 983044
  89.2 10.7 %collective-permute-start.4 = (f32[2,128,256]{1,2,0:T(8,128)S(1)}, f32[2,128,256]{1,2,0:T(8,128)S(1)}, u32[]{:S(2)}, u32[]{:S(2)}) collective-permute-start(f32[2,128,256]{1,2,0:T(8,128)S(1)} %get-tuple-element.5), channel_id=1, source_target_pairs={{0,32},{32,64},{64,96},{96,0},{1,33},{33,65},{65,97},{97,1},{2,34}... | collective-permute-start | bytes 786440 | tf_op jit(solution)/shard_map/ppermute | solution.py:15
  95.2 7.3 %collective-permute-start.5 = (f32[2,128,256]{1,2,0:T(8,128)S(1)}, f32[2,128,256]{1,2,0:T(8,128)S(1)}, u32[]{:S(2)}, u32[]{:S(2)}) collective-permute-start(f32[2,128,256]{1,2,0:T(8,128)S(1)} %get-tuple-element.6), channel_id=1, source_target_pairs={{32,0},{64,32},{96,64},{0,96},{33,1},{65,33},{97,65},{1,97},{34,2}... | collective-permute-start | bytes 786440 | tf_op jit(solution)/shard_map/ppermute | solution.py:18
where the time goes:
time: 107 us
  other arithmetic  29.4 us (27%)
  waiting for transfers between devices  28.9 us (27%)
  starting transfers between devices  27.4 us (26%)
  local copies, waits for them, and re-layouts  15.1 us (14%)
  matrix products  5.65 us (5%)
    scatter-add x1, other arithmetic, body(): jnp.zeros((whole,), jnp.float32).at[flat_index]  16.8 us
    ppermute x3, waiting for transfers between devices, with_halo(): lax.ppermute(lax.slice_in_dim(block, block.shape[dim] - width, None, axis...  16.5 us
    all_to_all x1, starting transfers between devices, body(): lax.all_to_all(send_cell, 'tile', split_axis=0, concat_axis=0, tiled=True)  11.2 us
    another operation x3, other arithmetic  9.15 us
    ppermute x3, starting transfers between devices, with_halo(): lax.ppermute(lax.slice_in_dim(block, block.shape[dim] - width, None, axis...  7.38 us
    all_to_all x1, waiting for transfers between devices, body(): lax.all_to_all(send_value, 'tile', split_axis=0, concat_axis=0, tiled=True)  7.29 us
    all_to_all x1, starting transfers between devices, body(): lax.all_to_all(send_value, 'tile', split_axis=0, concat_axis=0, tiled=True)  7.2 us
    dot_general x5, matrix products, body(): jnp.einsum('ij,djk->dik', lag_blocks[k], window, precision=lax.Precision....  4.95 us
  transfers between devices with their start and end apart: 8, of which 8 were waited for; matrix products, arithmetic and copies ran while one was open for 9% of the time, Pallas kernels for 0%

commit v1 on v0

v1 whole, which is shorter than its diff:
```python
import jax
import jax.numpy as jnp
from jax import lax
from jax.experimental import pallas as pl
from jax.experimental.pallas import tpu as pltpu
from jax.sharding import PartitionSpec as P

DAY_DEV = 8
LAT = 128
LON_DEV = 256
CAP = 96
LANES = 128
NTILE = 32
NYEAR = 4
NCLASS = 16
LAGS = 5
HALO = 2
DAYS_EXT = DAY_DEV + 2 * HALO
PAD = 8
F32 = jnp.float32
BF16 = jnp.bfloat16


def dot_nt(a, b):
    return lax.dot_general(a, b, (((1,), (1,)), ((), ())), preferred_element_type=F32)


def split2(x):
    hi = x.astype(BF16).astype(F32)
    return hi, x - hi


def hot(mask):
    return jnp.where(mask, 1.0, 0.0).astype(BF16)


def bucket(tile_ref, cell_ref, value_ref, pieces_ref, slots_ref, send_ref):
    tile = tile_ref[...]
    cell = cell_ref[...]
    hi, mid = split2(value_ref[...])
    day = jnp.right_shift(cell, 15).astype(F32)
    row = jnp.bitwise_and(jnp.right_shift(cell, 8), 127).astype(F32)
    col = jnp.bitwise_and(cell, 255).astype(F32)
    of_tile = lax.broadcasted_iota(jnp.int32, (NTILE, LANES), 0)
    masks = [tile[b : b + 1, :] == of_tile for b in range(8)]
    ones = jnp.concatenate([hot(m) for m in masks], axis=0)
    source = lax.broadcasted_iota(jnp.int32, (LANES, 2 * LANES), 0)
    target = lax.broadcasted_iota(jnp.int32, (LANES, 2 * LANES), 1)
    before = hot((source < target) | (target >= LANES))
    counts = jnp.dot(ones, before, preferred_element_type=F32)
    base = jnp.zeros((NTILE, LANES), F32)
    slot_iota = lax.broadcasted_iota(jnp.int32, (LANES, LANES), 0).astype(F32)
    for b in range(8):
        lanes = slice(b * LANES, (b + 1) * LANES)
        rank = counts[b * NTILE : (b + 1) * NTILE, :LANES] + base
        base = base + counts[b * NTILE : (b + 1) * NTILE, LANES:]
        slot = jnp.sum(jnp.where(masks[b], rank, 0.0), axis=0, keepdims=True)
        slots_ref[:, lanes] = hot(slot_iota == slot)
        for q, piece in enumerate((hi, mid, day, row, col)):
            pieces_ref[q * NTILE : (q + 1) * NTILE, lanes] = jnp.where(
                masks[b], piece[b : b + 1, :], 0.0
            ).astype(BF16)
    out = dot_nt(pieces_ref[...], slots_ref[...])
    part = [out[q * NTILE : (q + 1) * NTILE] for q in range(5)]
    send_ref[:, 0, :] = part[0] + part[1]
    send_ref[:, 1, :] = part[2] * 32768.0 + part[3] * 256.0 + part[4]


def dense(lists):
    a, b, c, d = (lists[8 * i : 8 * i + 8] for i in range(4))
    lane = lax.broadcasted_iota(jnp.int32, (8, LANES), 1)
    return jnp.concatenate(
        [
            jnp.where(lane < CAP, rows, pltpu.roll(d, shift, 1))
            for rows, shift in ((a, 96), (b, 64), (c, 32))
        ],
        axis=0,
    )


def spread_values(recv_ref, lhs_ref):
    hi, lo = split2(dense(recv_ref[:, 0, :]))
    cell = dense(recv_ref[:, 1, :]).astype(jnp.int32)
    day = jnp.right_shift(cell, 15)
    row = jnp.bitwise_and(jnp.right_shift(cell, 8), 127)
    col = jnp.bitwise_and(cell, 255)
    column = lax.broadcasted_iota(jnp.int32, (LON_DEV, LANES), 0)
    for k in range(24):
        lanes = slice(k * LANES, (k + 1) * LANES)
        here = col[k : k + 1, :] == column
        lhs_ref[:LON_DEV, lanes] = jnp.where(here, hi[k : k + 1, :], 0.0).astype(BF16)
        lhs_ref[LON_DEV:, lanes] = jnp.where(here, lo[k : k + 1, :], 0.0).astype(BF16)
    return day, row


def scatter_days(day, row, first, lhs_ref, rhs_ref):
    latitude = lax.broadcasted_iota(jnp.int32, (LAT, LANES), 0)
    for i in range(2):
        wanted = jnp.where(day == first + i, row, -1)
        for k in range(24):
            rhs_ref[i * LAT : (i + 1) * LAT, k * LANES : (k + 1) * LANES] = hot(
                wanted[k : k + 1, :] == latitude
            )
    both = dot_nt(lhs_ref[...], rhs_ref[...])
    return both[:LON_DEV] + both[LON_DEV:]


def kernel(
    tile_ref,
    cell_ref,
    value_ref,
    class_ref,
    coeff_ref,
    lag_ref,
    out_ref,
    pieces_ref,
    slots_ref,
    send_ref,
    recv_own,
    recv_prev,
    recv_next,
    class_t,
    class_halo,
    coef_ref,
    lhs_ref,
    rhs_ref,
    field,
    once,
    edge_own,
    edge_halo,
    got_own,
    got_halo,
    mix_ref,
    smooth_hi,
    smooth_lo,
    list_send,
    list_recv,
    year_send,
    year_recv,
    class_send,
    class_recv,
    edge_send,
    edge_recv,
):
    segment = lax.axis_index("year")
    me = lax.axis_index("tile")
    after = lax.rem(segment + 1, NYEAR)
    ahead = lax.rem(segment + NYEAR - 1, NYEAR)
    east = lax.rem(me + 1, NTILE)
    west = lax.rem(me + NTILE - 1, NTILE)

    barrier = pltpu.get_barrier_semaphore()

    @pl.loop(1, NTILE)
    def _(i):
        pl.semaphore_signal(barrier, inc=1, device_id={"tile": lax.rem(me + i, NTILE)})

    pl.semaphore_signal(barrier, inc=1, device_id={"year": after})
    pl.semaphore_signal(barrier, inc=1, device_id={"year": ahead})

    bucket(tile_ref, cell_ref, value_ref, pieces_ref, slots_ref, send_ref)
    class_t[...] = jnp.transpose(class_ref[...])

    pl.semaphore_wait(barrier, NTILE + 1)

    @pl.loop(1, NTILE)
    def _(i):
        tgt = lax.rem(me + i, NTILE)
        pltpu.make_async_remote_copy(
            send_ref.at[tgt], recv_own.at[i], list_send, list_recv, device_id={"tile": tgt}
        ).start()

    recv_own[0] = send_ref[me]
    class_copies = [
        pltpu.make_async_remote_copy(
            class_t.at[pl.ds(start, PAD)],
            class_halo.at[1 - side],
            class_send.at[side],
            class_recv.at[1 - side],
            device_id={"tile": tgt},
        )
        for side, start, tgt in ((0, 0, west), (1, LON_DEV - PAD, east))
    ]
    for copy in class_copies:
        copy.start()

    mix_ref[...] = jnp.zeros_like(mix_ref)
    for k in range(LAGS):
        hi, lo = split2(lag_ref[k])
        for i in range(2):
            lanes = slice((k + i) * LAT, (k + i + 1) * LAT)
            mix_ref[i * LAT : (i + 1) * LAT, lanes] = hi.astype(BF16)
            mix_ref[(2 + i) * LAT : (3 + i) * LAT, lanes] = lo.astype(BF16)

    def coefficients(ids, rows):
        kappa = hzon = hmer = jnp.zeros(ids.shape, F32)
        for c in range(NCLASS):
            here = ids == c
            kappa = jnp.where(here, coeff_ref[0, c], kappa)
            hzon = jnp.where(here, coeff_ref[1, c], hzon)
            hmer = jnp.where(here, coeff_ref[2, c], hmer)
        lane = lax.broadcasted_iota(jnp.int32, ids.shape, 1)
        coef_ref[0, rows] = kappa + 2.0 * hzon + 2.0 * hmer
        coef_ref[1, rows] = hzon
        coef_ref[2, rows] = jnp.where(lane < LAT - 1, hmer, 0.0)
        coef_ref[3, rows] = jnp.where(lane > 0, hmer, 0.0)

    coefficients(class_t[...], slice(PAD, PAD + LON_DEV))
    for copy in class_copies:
        copy.wait()
    coefficients(class_halo[0], slice(0, PAD))
    coefficients(class_halo[1], slice(PAD + LON_DEV, 2 * PAD + LON_DEV))

    everything = pltpu.make_async_remote_copy(
        send_ref.at[pl.ds(1, NTILE - 1)],
        recv_own.at[pl.ds(1, NTILE - 1)],
        list_send,
        list_recv,
        device_id={"tile": east},
    )
    everything.wait_recv()
    year_copies = [
        pltpu.make_async_remote_copy(
            recv_own, target, year_send.at[i], year_recv.at[i], device_id={"year": tgt}
        )
        for i, (target, tgt) in enumerate(((recv_prev, after), (recv_next, ahead)))
    ]
    for copy in year_copies:
        copy.start()

    def place(both, first, edges, at):
        for i in range(2):
            plane = both[:, i * LAT : (i + 1) * LAT]
            field[first + i, PAD : PAD + LON_DEV] = plane
            edges[0, at + 2 * i : at + 2 * i + 2] = plane[:2]
            edges[1, at + 2 * i : at + 2 * i + 2] = plane[LON_DEV - 2 :]

    def exchange(edges, got, which):
        copies = [
            pltpu.make_async_remote_copy(
                edges.at[side],
                got.at[1 - side],
                edge_send.at[which, side],
                edge_recv.at[which, 1 - side],
                device_id={"tile": tgt},
            )
            for side, tgt in ((0, west), (1, east))
        ]
        for copy in copies:
            copy.start()
        return copies

    day, row = spread_values(recv_own, lhs_ref)
    for pair in range(DAY_DEV // 2):
        both = scatter_days(day, row, 2 * pair, lhs_ref, rhs_ref)
        place(both, HALO + 2 * pair, edge_own, 4 * pair)
    own_copies = exchange(edge_own, got_own, 0)
    for i, (source, days, first) in enumerate(
        ((recv_prev, DAY_DEV - HALO, 0), (recv_next, 0, HALO + DAY_DEV))
    ):
        year_copies[i].wait_recv()
        day, row = spread_values(source, lhs_ref)
        place(scatter_days(day, row, days, lhs_ref, rhs_ref), first, edge_halo, 4 * i)
    halo_copies = exchange(edge_halo, got_halo, 1)

    def stencil(src, at, rows):
        length = rows.stop - rows.start
        v = src[at + (rows,)]
        e = src[at + (slice(rows.start + 1, rows.stop + 1),)]
        w = src[at + (slice(rows.start - 1, rows.stop - 1),)]
        north = pltpu.roll(v, LAT - 1, 1)
        south = pltpu.roll(v, 1, 1)
        return (
            coef_ref[0, rows] * v
            - coef_ref[1, rows] * (e + w)
            - coef_ref[2, rows] * north
            - coef_ref[3, rows] * south
        )

    def smooth(e, got, at):
        field[e, PAD - 2 : PAD] = got[0, at : at + 2]
        field[e, PAD + LON_DEV : PAD + LON_DEV + 2] = got[1, at : at + 2]
        for rows in (
            slice(PAD, PAD + LON_DEV),
            slice(PAD - 1, PAD),
            slice(PAD + LON_DEV, PAD + LON_DEV + 1),
        ):
            once[rows] = stencil(field, (e,), rows)
        twice = stencil(once, (), slice(PAD, PAD + LON_DEV))
        hi, lo = split2(twice)
        smooth_hi[:, e * LAT : (e + 1) * LAT] = hi.astype(BF16)
        smooth_lo[:, e * LAT : (e + 1) * LAT] = lo.astype(BF16)

    for copy in own_copies:
        copy.wait()
    for d in range(DAY_DEV):
        smooth(HALO + d, got_own, 2 * d)
    for copy in halo_copies:
        copy.wait()
    for i, e in enumerate((0, 1, HALO + DAY_DEV, HALO + DAY_DEV + 1)):
        smooth(e, got_halo, 2 * i)

    for pair in range(DAY_DEV // 2):
        window = slice(2 * pair * LAT, (2 * pair + LAGS + 1) * LAT)
        first = dot_nt(mix_ref[...], smooth_hi[:, window])
        second = dot_nt(mix_ref[: 2 * LAT], smooth_lo[:, window])
        mixed = first[: 2 * LAT] + (first[2 * LAT :] + second)
        out_ref[2 * pair] = mixed[:LAT]
        out_ref[2 * pair + 1] = mixed[LAT:]

    everything.wait_send()
    for copy in year_copies:
        copy.wait_send()


def body(station_tile, station_cell, station_value, class_ids, coeff_table, lag_blocks):
    vmem = pl.BlockSpec(memory_space=pltpu.VMEM)
    smem = pl.BlockSpec(memory_space=pltpu.SMEM)
    dma = pltpu.SemaphoreType.DMA
    slots = NTILE * CAP
    return pl.pallas_call(
        kernel,
        out_shape=jax.ShapeDtypeStruct((DAY_DEV, LAT, LON_DEV), F32),
        in_specs=[vmem, vmem, vmem, vmem, smem, vmem],
        out_specs=vmem,
        scratch_shapes=[
            pltpu.VMEM((5 * NTILE, 8 * LANES), BF16),
            pltpu.VMEM((LANES, 8 * LANES), BF16),
            pltpu.VMEM((NTILE, 2, LANES), F32),
            pltpu.VMEM((NTILE, 2, LANES), F32),
            pltpu.VMEM((NTILE, 2, LANES), F32),
            pltpu.VMEM((NTILE, 2, LANES), F32),
            pltpu.VMEM((LON_DEV, LAT), jnp.int32),
            pltpu.VMEM((2, PAD, LAT), jnp.int32),
            pltpu.VMEM((4, LON_DEV + 2 * PAD, LAT), F32),
            pltpu.VMEM((2 * LON_DEV, slots), BF16),
            pltpu.VMEM((2 * LAT, slots), BF16),
            pltpu.VMEM((DAYS_EXT, LON_DEV + 2 * PAD, LAT), F32),
            pltpu.VMEM((LON_DEV + 2 * PAD, LAT), F32),
            pltpu.VMEM((2, 2 * DAY_DEV, LAT), F32),
            pltpu.VMEM((2, 4 * HALO, LAT), F32),
            pltpu.VMEM((2, 2 * DAY_DEV, LAT), F32),
            pltpu.VMEM((2, 4 * HALO, LAT), F32),
            pltpu.VMEM((4 * LAT, (LAGS + 1) * LAT), BF16),
            pltpu.VMEM((LON_DEV, DAYS_EXT * LAT), BF16),
            pltpu.VMEM((LON_DEV, DAYS_EXT * LAT), BF16),
            dma,
            dma,
            dma((2,)),
            dma((2,)),
            dma((2,)),
            dma((2,)),
            dma((2, 2)),
            dma((2, 2)),
        ],
        compiler_params=pltpu.CompilerParams(
            collective_id=0, has_side_effects=True, vmem_limit_bytes=40 * 2**20
        ),
    )(
        station_tile.reshape(8, LANES),
        station_cell.reshape(8, LANES),
        station_value.reshape(8, LANES),
        class_ids,
        coeff_table,
        lag_blocks,
    )


def solution(mesh):
    in_specs = (
        P(("year", "tile"), None),
        P(("year", "tile")),
        P(("year", "tile")),
        P(None, "tile"),
        P(),
        P(),
    )
    out_specs = P("year", None, "tile")
    return jax.shard_map(body, mesh=mesh, in_specs=in_specs, out_specs=out_specs, check_vma=False)
```

time: 107 us -> 38.9 us (0.36)
  the two profiles are of different devices: /device:TPU:1 before, /device:TPU:0 now
where the time goes in v1:
time: 38.9 us; the launch traced here: 38.6 us
  Pallas kernels  33 us (85%)
  local copies, waits for them, and re-layouts  5.59 us (14%)
    pallas_call x1, Pallas kernels, body(): pl.pallas_call(kernel, out_shape=jax.ShapeDtypeStruct((DAY_DEV, LAT, LON_...  33 us
    unnamed x13, local copies, waits for them, and re-layouts  5.59 us

profile of v1, /device:TPU:0, one launch (start us, length us, event | category | flops | bytes accessed | tf_op | source)
XLA Modules:
  0.0 38.6 jit_solution(96704139649172496)
XLA Ops:
  0.0 0.0 copy-start.2
  0.0 0.7 %copy-done.2 = s32[1024,1]{0,1:T(1,128)S(1)} copy-done((s32[1024,1]{0,1:T(1,128)S(1)}, s32[1024,1]{0,1:T(1,128)}, u32[]{:S(2)}) %copy-start.2) | copy-done | bytes 4120
  0.7 0.0 copy-start
  0.7 1.0 %copy-done = f32[5,128,128]{2,1,0:T(8,128)S(1)} copy-done((f32[5,128,128]{2,1,0:T(8,128)S(1)}, f32[5,128,128]{2,1,0:T(8,128)}, u32[]{:S(2)}) %copy-start) | copy-done | bytes 327704
  1.7 0.0 copy-start.1
  1.7 0.9 %copy-done.1 = s32[128,256]{1,0:T(8,128)S(1)} copy-done((s32[128,256]{1,0:T(8,128)S(1)}, s32[128,256]{1,0:T(8,128)}, u32[]{:S(2)}) %copy-start.1) | copy-done | bytes 131096
  2.6 0.0 copy-start.3
  2.6 0.7 %copy-done.3 = s32[1024]{0:T(1024)S(1)} copy-done((s32[1024]{0:T(1024)S(1)}, s32[1024]{0:T(1024)}, u32[]{:S(2)}) %copy-start.3) | copy-done | bytes 4120
  3.3 0.0 copy-start.4
  3.3 0.7 %copy-done.4 = f32[1024]{0:T(1024)S(1)} copy-done((f32[1024]{0:T(1024)S(1)}, f32[1024]{0:T(1024)}, u32[]{:S(2)}) %copy-start.4) | copy-done | bytes 4120
  3.9 0.0 copy-start.5
  3.9 0.7 %copy-done.5 = f32[3,16]{1,0:T(4,128)S(1)} copy-done((f32[3,16]{1,0:T(4,128)S(1)}, f32[3,16]{1,0:T(4,128)}, u32[]{:S(2)}) %copy-start.5) | copy-done | bytes 216
  4.6 33.0 %shard_map.64 = f32[8,128,256]{2,1,0:T(8,128)S(1)} custom-call(s32[8,128]{1,0:T(8,128)S(1)} %bitcast.3, s32[8,128]{1,0:T(8,128)S(1)} %bitcast.4, f32[8,128]{1,0:T(8,128)S(1)} %bitcast.5, s32[128,256]{1,0:T(8,128)S(1)} %copy-done.1, f32[3,16]{1,0:T(4,128)S(1)} %copy-done.5, f32[5,128,128]{2,1,0:T(8,128)S(1)} %copy-done), custom_call_target="tpu_custom_call" | custom-call | tf_op jit(solution)/shard_map/pallas_call | solution.py:321
  37.6 1.0 %copy.8 = f32[8,128,256]{2,1,0:T(8,128)} copy(f32[8,128,256]{2,1,0:T(8,128)S(1)} %shard_map.64) | data formatting | bytes 2097152
Async XLA Ops:
  0.0 0.7 %copy-start.2 = (s32[1024,1]{0,1:T(1,128)S(1)}, s32[1024,1]{0,1:T(1,128)}, u32[]{:S(2)}) copy-start(s32[1024,1]{0,1:T(1,128)} %param.6) | copy-start | bytes 12292
  0.7 1.0 %copy-start = (f32[5,128,128]{2,1,0:T(8,128)S(1)}, f32[5,128,128]{2,1,0:T(8,128)}, u32[]{:S(2)}) copy-start(f32[5,128,128]{2,1,0:T(8,128)} %lag_ref.1) | copy-start | bytes 983044
  1.7 0.9 %copy-start.1 = (s32[128,256]{1,0:T(8,128)S(1)}, s32[128,256]{1,0:T(8,128)}, u32[]{:S(2)}) copy-start(s32[128,256]{1,0:T(8,128)} %class_ref.1) | copy-start | bytes 393220
  2.6 0.7 %copy-start.3 = (s32[1024]{0:T(1024)S(1)}, s32[1024]{0:T(1024)}, u32[]{:S(2)}) copy-start(s32[1024]{0:T(1024)} %param.7) | copy-start | bytes 12292
  3.3 0.7 %copy-start.4 = (f32[1024]{0:T(1024)S(1)}, f32[1024]{0:T(1024)}, u32[]{:S(2)}) copy-start(f32[1024]{0:T(1024)} %param.8) | copy-start | bytes 12292
  3.9 0.7 %copy-start.5 = (f32[3,16]{1,0:T(4,128)S(1)}, f32[3,16]{1,0:T(4,128)}, u32[]{:S(2)}) copy-start(f32[3,16]{1,0:T(4,128)} %coeff_ref.1) | copy-start | bytes 580
